TPU v7x, 32 devices: a whole 2x2x4 slice. The times are simulated.
32 devices in a mesh: blk: 4 (over y, x), row: 8 (over z, core).
Axes of the slice: x: 2, y: 2, z: 4, core: 2. Of those that a mesh axis runs over, the one named last changes fastest.
Arguments:
- intersection: bfloat16 [2048, 2048], P('row', 'blk'), may hold values from -0.125 to 0.125
- inverse_dev: bfloat16 [2048, 2048], P('row', 'blk'), may hold values from -0.125 to 0.125
- hamiltonian: bfloat16 [2048, 2048], P('row', 'blk'), may hold values from -0.09375 to 0.09375
- chem_potential: float32 [1], replicated, may hold values from -0.4 to 0.4
- pattern_s: int32 [16, 16], replicated, may hold values 0 or 1
- pattern_z: int32 [16, 16], replicated, may hold values 0 or 1
- pattern_h: int32 [16, 16], replicated, may hold values 0 or 1
- fill_inverse: int32 [16, 16], replicated, may hold values 0 or 1
- fill_sign: int32 [16, 16], replicated, may hold values 0 or 1
Outputs:
- refined_inverse: bfloat16 [2048, 2048], P('row', 'blk')
- inverse_error: bfloat16 [2048, 2048], P('row', 'blk')
- sign_step: bfloat16 [2048, 2048], P('row', 'blk')
All inputs are finite; a program needn't handle non-finite values.
Results may differ from a plain program's by a relative error of at most 0.0067.
Values may be sent and summed in bfloat16 or wider, within the bound.
A program may use at most 64 MiB of HBM per device.

v0:
```python
import jax
import jax.numpy as jnp
from jax import lax
from jax.sharding import PartitionSpec as P

BS = 128


def expand_local(pattern, row_start, rows, col_start, cols):
    count = pattern.shape[0]
    labels = jnp.arange(count, dtype=jnp.int32)
    row_blocks = (row_start + jnp.arange(rows, dtype=jnp.int32)) // BS
    col_blocks = (col_start + jnp.arange(cols, dtype=jnp.int32)) // BS
    row_pick = (row_blocks[:, None] == labels[None, :]).astype(jnp.float32)
    col_pick = (col_blocks[:, None] == labels[None, :]).astype(jnp.float32)
    inner = jnp.dot(row_pick, pattern.astype(jnp.float32), precision=lax.Precision.HIGHEST)
    return jnp.dot(inner, col_pick.T, precision=lax.Precision.HIGHEST)


def make_folder(panel, piece):
    return jnp.dot(panel, piece, preferred_element_type=jnp.float32)


def body(
    intersection,
    inverse_dev,
    hamiltonian,
    chem_potential,
    pattern_s,
    pattern_z,
    pattern_h,
    fill_inverse,
    fill_sign,
):
    rows, cols = intersection.shape
    row_start = lax.axis_index("row") * rows
    col_start = lax.axis_index("blk") * cols
    ident = (
        (row_start + jnp.arange(rows, dtype=jnp.int32))[:, None]
        == (col_start + jnp.arange(cols, dtype=jnp.int32))[None, :]
    ).astype(jnp.float32)
    seff = (
        ident
        + 0.35
        * expand_local(pattern_s, row_start, rows, col_start, cols)
        * intersection.astype(jnp.float32)
    ).astype(jnp.bfloat16)
    zeff = (
        ident
        - 0.35
        * expand_local(pattern_z, row_start, rows, col_start, cols)
        * inverse_dev.astype(jnp.float32)
    ).astype(jnp.bfloat16)
    heff = (
        expand_local(pattern_h, row_start, rows, col_start, cols) * hamiltonian.astype(jnp.float32)
    ).astype(jnp.bfloat16)
    z_rows = lax.all_gather(zeff, "blk", axis=1, tiled=True)
    s_cols = lax.all_gather(seff, "row", axis=0, tiled=True)
    first = jnp.dot(z_rows, s_cols, preferred_element_type=jnp.float32).astype(jnp.bfloat16)
    f_rows = lax.all_gather(first, "blk", axis=1, tiled=True)
    second = make_folder(f_rows, lax.all_gather(zeff, "row", axis=0, tiled=True))
    keep_inverse = expand_local(fill_inverse, row_start, rows, col_start, cols)
    refined = (keep_inverse * (2.0 * zeff.astype(jnp.float32) - second)).astype(jnp.bfloat16)
    r_rows = lax.all_gather(refined, "blk", axis=1, tiled=True)
    error = (ident - jnp.dot(r_rows, s_cols, preferred_element_type=jnp.float32)).astype(
        jnp.bfloat16
    )
    third = make_folder(r_rows, lax.all_gather(heff, "row", axis=0, tiled=True))
    keep_sign = expand_local(fill_sign, row_start, rows, col_start, cols)
    shifted = (keep_sign * third - chem_potential[0] * ident).astype(jnp.bfloat16)
    x_rows = lax.all_gather(shifted, "blk", axis=1, tiled=True)
    squared = make_folder(x_rows, lax.all_gather(shifted, "row", axis=0, tiled=True))
    square = (keep_sign * squared).astype(jnp.bfloat16)
    cube = make_folder(x_rows, lax.all_gather(square, "row", axis=0, tiled=True))
    sign = (0.5 * (3.0 * shifted.astype(jnp.float32) - cube)).astype(jnp.bfloat16)
    return (refined, error, sign)


def solution(mesh):
    placed = (P("row", "blk"), P("row", "blk"), P("row", "blk"), P(), P(), P(), P(), P(), P())
    return jax.shard_map(
        body,
        mesh=mesh,
        in_specs=placed,
        out_specs=(P("row", "blk"), P("row", "blk"), P("row", "blk")),
        check_vma=False,
    )
```

profile of v0, /device:TPU:1, one launch (start us, length us, event | category | flops | bytes accessed | tf_op | source)
XLA Modules:
  0.0 291.8 jit_solution(18002602931997322105)
XLA Ops:
  7.2 0.0 all-gather.10.cloned.1.call-start
  7.3 1.0 fusion.25
  8.2 2.2 fusion.13
  10.4 0.0 all-gather.10.cloned.1.call-update
  10.5 0.0 all-gather.12.cloned.1.call-start
  10.5 1.0 fusion.24
  11.5 2.2 fusion.12
  13.7 0.0 all-gather.12.cloned.1.call-update
  13.7 0.0 copy-start.4
  13.7 0.0 all-gather.16.cloned.1.call-start
  13.7 0.7 all-gather.16.cloned.1.call-update
  14.4 0.0 copy-start.3
  14.4 0.0 copy-start.5
  14.5 0.0 copy-start
  14.5 0.0 all-gather.14.cloned.1.call-start
  14.5 24.7 %all-gather.10.cloned.1.call-done = bf16[256,2048]{1,0:T(8,128)(2,1)} async-done(((bf16[256,512]{1,0:T(8,128)(2,1)}), bf16[256,2048]{1,0:T(8,128)(2,1)}) %all-gather.10.cloned.1.call-update) | async-done | bytes 1048592 | tf_op jit(solution)/shard_map/all_gather | solution.py:57
  39.2 31.7 %all-gather.12.cloned.1.call-done = bf16[2048,512]{1,0:T(8,128)(2,1)} async-done(((bf16[256,512]{1,0:T(8,128)(2,1)}), bf16[2048,512]{1,0:T(8,128)(2,1)}) %all-gather.12.cloned.1.call-update) | async-done | bytes 2097168 | tf_op jit(solution)/shard_map/all_gather | solution.py:58
  70.9 3.3 %convolution_convert_fusion = bf16[256,512]{1,0:T(8,128)(2,1)} fusion(bf16[256,2048]{1,0:T(8,128)(2,1)} %all-gather.10.cloned.1.call-done, bf16[2048,512]{1,0:T(8,128)(2,1)} %all-gather.12.cloned.1.call-done), kind=kOutput, calls=%fused_computation.23 | convolution fusion | flops 537001984 | bytes 3407872 | tf_op jit(solution)/shard_map/dot_general | solution.py:59
  74.2 0.0 all-gather.14.cloned.1.call-update
  74.2 0.0 all-gather.20.cloned.1.call-start
  74.3 0.3 fusion.22
  74.6 1.2 fusion.14
  75.8 0.0 all-gather.20.cloned.1.call-update
  75.8 0.0 all-gather.18.cloned.1.call-start
  75.9 0.3 fusion.26
  76.1 0.5 fusion.16
  76.6 0.0 copy-start.6
  76.6 25.1 %all-gather.16.cloned.1.call-done = bf16[2048,512]{1,0:T(8,128)(2,1)} async-done(((bf16[256,512]{1,0:T(8,128)(2,1)}), bf16[2048,512]{1,0:T(8,128)(2,1)}) %all-gather.16.cloned.1.call-update) | async-done | bytes 2097168 | tf_op jit(solution)/shard_map/all_gather | solution.py:61
  101.7 27.9 %all-gather.14.cloned.1.call-done = bf16[256,2048]{1,0:T(8,128)(2,1)} async-done(((bf16[256,512]{1,0:T(8,128)(2,1)}), bf16[256,2048]{1,0:T(8,128)(2,1)}) %all-gather.14.cloned.1.call-update) | async-done | bytes 1048592 | tf_op jit(solution)/shard_map/all_gather | solution.py:60
  129.6 3.3 %fusion.7 = bf16[256,512]{1,0:T(8,128)(2,1)} fusion(f32[256,512]{1,0:T(8,128)S(1)} %fusion.16, bf16[256,2048]{1,0:T(8,128)(2,1)} %all-gather.14.cloned.1.call-done, bf16[2048,512]{1,0:T(8,128)(2,1)} %all-gather.16.cloned.1.call-done, bf16[256,512]{1,0:T(8,128)(2,1)S(1)} %copy-done), kind=kOutput, calls=%fused_computation.15 | convolution fusion | flops 537526272 | bytes 4194304 | tf_op jit(solution)/shard_map/dot_general | solution.py:21
  132.9 0.0 all-gather.18.cloned.1.call-update
  132.9 0.0 all-gather.22.cloned.1.call-start
  133.6 0.3 fusion.23
  133.9 0.5 fusion.15
  134.4 26.2 %all-gather.20.cloned.1.call-done = bf16[2048,512]{1,0:T(8,128)(2,1)} async-done(((bf16[256,512]{1,0:T(8,128)(2,1)}), bf16[2048,512]{1,0:T(8,128)(2,1)}) %all-gather.20.cloned.1.call-update) | async-done | bytes 2097168 | tf_op jit(solution)/shard_map/all_gather | solution.py:68
  160.6 27.9 %all-gather.18.cloned.1.call-done = bf16[256,2048]{1,0:T(8,128)(2,1)} async-done(((bf16[256,512]{1,0:T(8,128)(2,1)}), bf16[256,2048]{1,0:T(8,128)(2,1)}) %all-gather.18.cloned.1.call-update) | async-done | bytes 1048592 | tf_op jit(solution)/shard_map/all_gather | solution.py:64
  188.4 3.3 %fusion.9 = bf16[256,512]{1,0:T(8,128)(2,1)} fusion(f32[256,512]{1,0:T(8,128)S(1)} %fusion.15, bf16[256,2048]{1,0:T(8,128)(2,1)} %all-gather.18.cloned.1.call-done, bf16[2048,512]{1,0:T(8,128)(2,1)} %all-gather.20.cloned.1.call-done, f32[]{:T(128)} %bitcast.18, s32[512]{0:T(512)S(1)} %iota_add_fusion, s32[256]{0:T(256)S(1)} %iota_add_fusion.1), kind=kOutput, calls=%fused_computation.17 | convolution fusion | flops 537526272 | bytes 3935236 | tf_op jit(solution)/shard_map/dot_general | solution.py:21
  191.8 0.0 all-gather.22.cloned.1.call-update
  191.8 0.0 all-gather.24.cloned.1.call-start
  191.8 0.7 all-gather.24.cloned.1.call-update
  192.6 0.0 all-gather.26.cloned.1.call-start
  192.6 25.8 %all-gather.22.cloned.1.call-done = bf16[256,2048]{1,0:T(8,128)(2,1)} async-done(((bf16[256,512]{1,0:T(8,128)(2,1)}), bf16[256,2048]{1,0:T(8,128)(2,1)}) %all-gather.22.cloned.1.call-update) | async-done | bytes 1048592 | tf_op jit(solution)/shard_map/all_gather | solution.py:71
  218.4 31.7 %all-gather.24.cloned.1.call-done = bf16[2048,512]{1,0:T(8,128)(2,1)} async-done(((bf16[256,512]{1,0:T(8,128)(2,1)}), bf16[2048,512]{1,0:T(8,128)(2,1)}) %all-gather.24.cloned.1.call-update) | async-done | bytes 2097168 | tf_op jit(solution)/shard_map/all_gather | solution.py:72
  250.2 3.3 %fusion.10 = bf16[256,512]{1,0:T(8,128)(2,1)} fusion(f32[256,512]{1,0:T(8,128)S(1)} %fusion.15, bf16[256,2048]{1,0:T(8,128)(2,1)} %all-gather.22.cloned.1.call-done, bf16[2048,512]{1,0:T(8,128)(2,1)} %all-gather.24.cloned.1.call-done), kind=kOutput, calls=%fused_computation.18 | convolution fusion | flops 537133056 | bytes 3932160 | tf_op jit(solution)/shard_map/dot_general | solution.py:21
  253.5 0.0 all-gather.26.cloned.1.call-update
  253.5 2.8 fusion.8
  256.3 26.0 %all-gather.26.cloned.1.call-done = bf16[2048,512]{1,0:T(8,128)(2,1)} async-done(((bf16[256,512]{1,0:T(8,128)(2,1)}), bf16[2048,512]{1,0:T(8,128)(2,1)}) %all-gather.26.cloned.1.call-update) | async-done | bytes 2097168 | tf_op jit(solution)/shard_map/all_gather | solution.py:74
  282.3 3.0 %fusion.11 = bf16[256,512]{1,0:T(8,128)(2,1)} fusion(bf16[256,2048]{1,0:T(8,128)(2,1)S(1)} %copy-done.2, bf16[2048,512]{1,0:T(8,128)(2,1)} %all-gather.26.cloned.1.call-done, bf16[256,512]{1,0:T(8,128)(2,1)S(1)} %copy-done.1), kind=kOutput, calls=%fused_computation.19 | convolution fusion | flops 537526272 | bytes 3670016 | tf_op jit(solution)/shard_map/dot_general | solution.py:21
  (15 shorter events, 0.1 us)
Async XLA Ops:
  7.2 32.0 %all-gather.10.cloned.1.call-start = ((), (), s32[]{:S(2)}) async-start(), calls=%async_computation | async-start | bytes 1310720 | tf_op jit(solution)/shard_map/all_gather | solution.py:57
  10.5 60.4 %all-gather.12.cloned.1.call-start = ((), (), s32[]{:S(2)}) async-start(), calls=%async_computation.1 | async-start | bytes 2359296 | tf_op jit(solution)/shard_map/all_gather | solution.py:58
  13.7 60.6 %copy-start.4 = (s32[16,16]{1,0:T(8,128)S(1)}, s32[16,16]{1,0:T(8,128)}, u32[]{:S(2)}) copy-start(s32[16,16]{1,0:T(8,128)} %param.15) | copy-start | bytes 3076
  13.7 88.0 %all-gather.16.cloned.1.call-start = ((), (), s32[]{:S(2)}) async-start(), calls=%async_computation.3 | async-start | bytes 2359296 | tf_op jit(solution)/shard_map/all_gather | solution.py:61
  14.4 60.1 %copy-start.3 = (bf16[256,512]{1,0:T(8,128)(2,1)S(1)}, bf16[256,512]{1,0:T(8,128)(2,1)}, u32[]{:S(2)}) copy-start(bf16[256,512]{1,0:T(8,128)(2,1)} %param.11) | copy-start | bytes 786436
  14.4 61.4 %copy-start.5 = (s32[16,16]{1,0:T(8,128)S(1)}, s32[16,16]{1,0:T(8,128)}, u32[]{:S(2)}) copy-start(s32[16,16]{1,0:T(8,128)} %param.16) | copy-start | bytes 3076
  14.5 115.1 %copy-start = (bf16[256,512]{1,0:T(8,128)(2,1)S(1)}, bf16[256,512]{1,0:T(8,128)(2,1)}, u32[]{:S(2)}) copy-start(bf16[256,512]{1,0:T(8,128)(2,1)} %fusion.13) | copy-start | bytes 786436
  14.5 115.1 %all-gather.14.cloned.1.call-start = ((), (), s32[]{:S(2)}) async-start(), calls=%async_computation.2 | async-start | bytes 1310720 | tf_op jit(solution)/shard_map/all_gather | solution.py:60
  74.2 86.3 %all-gather.20.cloned.1.call-start = ((), (), s32[]{:S(2)}) async-start(), calls=%async_computation.5 | async-start | bytes 2359296 | tf_op jit(solution)/shard_map/all_gather | solution.py:68
  75.8 112.6 %all-gather.18.cloned.1.call-start = ((), (), s32[]{:S(2)}) async-start(), calls=%async_computation.4 | async-start | bytes 1310720 | tf_op jit(solution)/shard_map/all_gather | solution.py:64
  76.6 57.0 %copy-start.6 = (s32[16,16]{1,0:T(8,128)S(1)}, s32[16,16]{1,0:T(8,128)}, u32[]{:S(2)}) copy-start(s32[16,16]{1,0:T(8,128)} %param.17) | copy-start | bytes 3076
  132.9 85.5 %all-gather.22.cloned.1.call-start = ((), (), s32[]{:S(2)}) async-start(), calls=%async_computation.6 | async-start | bytes 1310720 | tf_op jit(solution)/shard_map/all_gather | solution.py:71
  191.8 58.4 %all-gather.24.cloned.1.call-start = ((), (), s32[]{:S(2)}) async-start(), calls=%async_computation.7 | async-start | bytes 2359296 | tf_op jit(solution)/shard_map/all_gather | solution.py:72
  192.5 61.0 %copy-start.7 = (bf16[2048,512]{1,0:T(8,128)(2,1)S(1)}, bf16[2048,512]{1,0:T(8,128)(2,1)}, u32[]{:S(2)}) copy-start(bf16[2048,512]{1,0:T(8,128)(2,1)} %all-gather.12.cloned.1.call-done) | copy-start | bytes 6291460
  192.6 89.7 %all-gather.26.cloned.1.call-start = ((), (), s32[]{:S(2)}) async-start(), calls=%async_computation.8 | async-start | bytes 2359296 | tf_op jit(solution)/shard_map/all_gather | solution.py:74
  253.5 28.8 %copy-start.1 = (bf16[256,512]{1,0:T(8,128)(2,1)S(1)}, bf16[256,512]{1,0:T(8,128)(2,1)}, u32[]{:S(2)}) copy-start(bf16[256,512]{1,0:T(8,128)(2,1)} %fusion.9) | copy-start | bytes 786436
  253.5 28.8 %copy-start.2 = (bf16[256,2048]{1,0:T(8,128)(2,1)S(1)}, bf16[256,2048]{1,0:T(8,128)(2,1)}, u32[]{:S(2)}) copy-start(bf16[256,2048]{1,0:T(8,128)(2,1)} %all-gather.22.cloned.1.call-done) | copy-start | bytes 3145732
Sparse Core Ops, SparseCore 0:
  10.6 28.5 all-gather.9
  41.4 29.4 all-gather.11
  73.1 28.5 all-gather.15
  104.0 25.5 all-gather.13
  131.0 29.4 all-gather.19
  162.8 25.5 all-gather.17
  191.9 26.4 all-gather.21
  220.6 29.4 all-gather.23
  253.6 28.5 all-gather.25
where the time goes:
time: 292 us
  waiting for transfers between devices  248 us (85%)
  matrix products  28.4 us (10%)
  between operations  14.7 us (5%)
    all_gather x1, waiting for transfers between devices, body(): s_cols = lax.all_gather(seff, 'row', axis=0, tiled=True)  31.7 us
    all_gather x1, waiting for transfers between devices, body(): lax.all_gather(shifted, 'row', axis=0, tiled=True)  31.7 us
    all_gather x1, waiting for transfers between devices, body(): r_rows = lax.all_gather(refined, 'blk', axis=1, tiled=True)  27.9 us
    all_gather x1, waiting for transfers between devices, body(): f_rows = lax.all_gather(first, 'blk', axis=1, tiled=True)  27.9 us
    all_gather x1, waiting for transfers between devices, body(): third = make_folder(r_rows, lax.all_gather(heff, 'row', axis=0, tiled=True))  26.2 us
    all_gather x1, waiting for transfers between devices, body(): lax.all_gather(square, 'row', axis=0, tiled=True)  26 us
    all_gather x1, waiting for transfers between devices, body(): x_rows = lax.all_gather(shifted, 'blk', axis=1, tiled=True)  25.8 us
    all_gather x1, waiting for transfers between devices, body(): lax.all_gather(zeff, 'row', axis=0, tiled=True)  25.1 us
  transfers between devices with their start and end apart: 9, of which 9 were waited for; matrix products, arithmetic and copies ran while one was open for 5% of the time, Pallas kernels for 0%

commit v1 on v0

v1 whole, which is shorter than its diff:
```python
import functools

import jax
import jax.numpy as jnp
from jax import lax
from jax.experimental import pallas as pl
from jax.experimental.pallas import tpu as pltpu
from jax.sharding import PartitionSpec as P

BS = 128
MESH = pl.DeviceIdType.MESH
S, Z, H, X, Q = range(5)
ZR, FR, RR, XR = range(4)


def kernel(
    blks,
    rows_n,
    inter_ref,
    inv_ref,
    ham_ref,
    chem_ref,
    ps_ref,
    pz_ref,
    ph_ref,
    fi_ref,
    fs_ref,
    refined_ref,
    error_ref,
    sign_ref,
    cols,
    panels,
    acc,
    col_send,
    col_recv,
    row_send,
    row_recv,
):
    rows, width = inter_ref.shape
    chips = rows_n // 2
    chunk = 2 * rows
    per = width // chunk
    me_row = lax.axis_index("row")
    me_blk = lax.axis_index("blk")
    chip = me_row // 2
    core = me_row % 2
    mate = chip * 2 + (1 - core)

    def row_device(r):
        return {"row": r, "blk": me_blk}

    def blk_device(b):
        return {"row": me_row, "blk": b}

    def slot(i, r):
        return cols.at[i, pl.ds(pl.multiple_of(r * rows, rows), rows)]

    def col_copy(i, kind, c, target, source):
        return pltpu.make_async_remote_copy(
            src_ref=slot(i, source),
            dst_ref=slot(i, source),
            send_sem=col_send.at[i, kind, c],
            recv_sem=col_recv.at[i, source],
            device_id=row_device(target),
            device_id_type=MESH,
        )

    def mine(c):
        return c * 2 + core

    def up(i, c):
        return col_copy(i, 0, c, me_row + 2, mine(c))

    def down(i, c):
        return col_copy(i, 1, c, me_row - 2, mine(c))

    def across(i, c):
        return col_copy(i, 2, c, mate, mine(c))

    def from_mate(i, c):
        return col_copy(i, 2, c, mate, c * 2 + (1 - core))

    def row_copy(i, step):
        to = lax.rem(me_blk + step, blks)
        return pltpu.make_async_remote_copy(
            src_ref=panels.at[i, me_blk],
            dst_ref=panels.at[i, me_blk],
            send_sem=row_send.at[i, step],
            recv_sem=row_recv.at[i, me_blk],
            device_id=blk_device(to),
            device_id_type=MESH,
        )

    def row_arrival(i, step):
        source = lax.rem(me_blk + step, blks)
        return pltpu.make_async_remote_copy(
            src_ref=panels.at[i, source],
            dst_ref=panels.at[i, source],
            send_sem=row_send.at[i, step],
            recv_sem=row_recv.at[i, source],
            device_id=blk_device(source),
            device_id_type=MESH,
        )

    def send_rows(i):
        for step in range(1, blks):
            row_copy(i, step).start()

    def wait_rows(i):
        for step in range(1, blks):
            row_arrival(i, step).wait_recv()

    def send_own(i):
        @pl.when(chip + 1 < chips)
        def _():
            up(i, chip).start()

        @pl.when(chip > 0)
        def _():
            down(i, chip).start()

        across(i, chip).start()

    def relay(i, d):
        @pl.when(chip - d >= 0)
        def _():
            c = chip - d
            up(i, c).wait_recv()

            @pl.when(chip + 1 < chips)
            def _():
                up(i, c).start()

            across(i, c).start()

        @pl.when(chip + d < chips)
        def _():
            c = chip + d
            down(i, c).wait_recv()

            @pl.when(chip > 0)
            def _():
                down(i, c).start()

            across(i, c).start()

    def term(i, a, c):
        left = panels[a, c // per] if per == 1 else panels[a, c // per, :, pl.ds(pl.multiple_of(c % per * chunk, chunk), chunk)]
        right = cols[i, pl.ds(pl.multiple_of(c * chunk, chunk), chunk)]
        return jnp.dot(left, right, preferred_element_type=jnp.float32)

    def fold(i, a, d):
        @pl.when(chip - d >= 0)
        def _():
            c = chip - d
            from_mate(i, c).wait_recv()
            acc[...] += term(i, a, c)

        @pl.when(chip + d < chips)
        def _():
            c = chip + d
            from_mate(i, c).wait_recv()
            acc[...] += term(i, a, c)

    def loop(low, high, f):
        def step(d, carry):
            f(d)
            return carry

        lax.fori_loop(low, high, step, 0)

    def column_pass(i, a, after, fresh=True):
        loop(1, chips - 1, lambda d: relay(i, d))
        after()
        if fresh:
            wait_rows(a)
        from_mate(i, chip).wait_recv()
        acc[...] = term(i, a, chip)
        loop(1, chips - 1, lambda d: fold(i, a, d))
        if chips > 1:
            relay(i, chips - 1)
            fold(i, a, chips - 1)

    tall, wide = rows // BS, width // BS

    def tiles(f):
        for p in range(tall):
            for q in range(wide):
                f(p, q, (slice(p * BS, (p + 1) * BS), slice(q * BS, (q + 1) * BS)))

    def keep(ref, p, q):
        return ref[me_row * tall + p, me_blk * wide + q].astype(jnp.float32)

    def ident(p, q):
        gap = (me_blk * width + q * BS) - (me_row * rows + p * BS)
        i = lax.broadcasted_iota(jnp.int32, (BS, BS), 0)
        j = lax.broadcasted_iota(jnp.int32, (BS, BS), 1)
        return jnp.where(i - j == gap, 1.0, 0.0).astype(jnp.float32)

    def put_col(i, p, q, value):
        cols[
            i,
            pl.ds(pl.multiple_of(me_row * rows + p * BS, BS), BS),
            q * BS : (q + 1) * BS,
        ] = value

    def put_row(a, p, q, value):
        panels[a, me_blk, p * BS : (p + 1) * BS, q * BS : (q + 1) * BS] = value

    def make_s(p, q, at):
        value = ident(p, q) + 0.35 * keep(ps_ref, p, q) * inter_ref[at].astype(jnp.float32)
        put_col(S, p, q, value.astype(jnp.bfloat16))

    def make_z(p, q, at):
        value = ident(p, q) - 0.35 * keep(pz_ref, p, q) * inv_ref[at].astype(jnp.float32)
        value = value.astype(jnp.bfloat16)
        put_col(Z, p, q, value)
        put_row(ZR, p, q, value)

    def make_h(p, q, at):
        value = keep(ph_ref, p, q) * ham_ref[at].astype(jnp.float32)
        put_col(H, p, q, value.astype(jnp.bfloat16))

    def make_refined(p, q, at):
        own = panels[ZR, me_blk, at[0], at[1]].astype(jnp.float32)
        value = (keep(fi_ref, p, q) * (2.0 * own - acc[at])).astype(jnp.bfloat16)
        put_row(RR, p, q, value)
        refined_ref[at] = value

    def make_x(p, q, at):
        value = keep(fs_ref, p, q) * acc[at] - chem_ref[0] * ident(p, q)
        value = value.astype(jnp.bfloat16)
        put_col(X, p, q, value)
        put_row(XR, p, q, value)

    def make_q(p, q, at):
        put_col(Q, p, q, (keep(fs_ref, p, q) * acc[at]).astype(jnp.bfloat16))

    def make_error(p, q, at):
        error_ref[at] = (ident(p, q) - acc[at]).astype(jnp.bfloat16)

    def make_sign(p, q, at):
        own = panels[XR, me_blk, at[0], at[1]].astype(jnp.float32)
        sign_ref[at] = (0.5 * (3.0 * own - acc[at])).astype(jnp.bfloat16)

    barrier = pltpu.get_barrier_semaphore()

    def greet(device):
        pl.semaphore_signal(barrier, inc=1, device_id=device, device_id_type=MESH)

    greet(row_device(mate))
    for step in range(1, blks):
        greet(blk_device(lax.rem(me_blk + step, blks)))

    @pl.when(chip + 1 < chips)
    def _():
        greet(row_device(me_row + 2))

    @pl.when(chip > 0)
    def _():
        greet(row_device(me_row - 2))

    tiles(make_s)
    tiles(make_z)
    above = jnp.where(chip + 1 < chips, 1, 0)
    below = jnp.where(chip > 0, 1, 0)
    pl.semaphore_wait(barrier, blks + above + below)

    send_own(S)
    send_rows(ZR)
    tiles(make_h)

    column_pass(S, ZR, lambda: send_own(Z))
    panels[FR, me_blk] = acc[...].astype(jnp.bfloat16)
    send_rows(FR)

    column_pass(Z, FR, lambda: send_own(H))
    tiles(make_refined)
    send_rows(RR)

    column_pass(H, RR, lambda: None)
    tiles(make_x)
    send_own(X)
    send_rows(XR)

    def error_product():
        acc[...] = jnp.zeros_like(acc)

        def add(c):
            acc[...] += term(S, RR, c)

        loop(0, chips, add)
        tiles(make_error)

    column_pass(X, XR, error_product)
    tiles(make_q)
    send_own(Q)
    column_pass(Q, XR, lambda: None, fresh=False)
    tiles(make_sign)

    for i in range(5):

        def drain(c, i=i):
            @pl.when((chip + 1 < chips) & (c <= chip))
            def _():
                up(i, c).wait_send()

            @pl.when((chip > 0) & (c >= chip))
            def _():
                down(i, c).wait_send()

            across(i, c).wait_send()

        loop(0, chips, drain)
    for i in range(4):
        for step in range(1, blks):
            row_copy(i, step).wait_send()


def body(blks, rows_n, *args):
    rows, width = args[0].shape
    out = jax.ShapeDtypeStruct((rows, width), jnp.bfloat16)
    vmem = pl.BlockSpec(memory_space=pltpu.VMEM)
    smem = pl.BlockSpec(memory_space=pltpu.SMEM)
    depth = rows_n * rows
    return pl.pallas_call(
        functools.partial(kernel, blks, rows_n),
        out_shape=(out, out, out),
        in_specs=[vmem] * 3 + [smem] * 6,
        out_specs=(vmem, vmem, vmem),
        scratch_shapes=[
            pltpu.VMEM((5, depth, width), jnp.bfloat16),
            pltpu.VMEM((4, blks, rows, width), jnp.bfloat16),
            pltpu.VMEM((rows, width), jnp.float32),
            pltpu.SemaphoreType.DMA((5, 3, rows_n // 2)),
            pltpu.SemaphoreType.DMA((5, rows_n)),
            pltpu.SemaphoreType.DMA((4, blks)),
            pltpu.SemaphoreType.DMA((4, blks)),
        ],
        compiler_params=pltpu.CompilerParams(
            collective_id=0, has_side_effects=True, vmem_limit_bytes=48 * 1024 * 1024
        ),
        cost_estimate=pl.CostEstimate(
            flops=12 * rows * depth * width, bytes_accessed=12 * rows * width, transcendentals=0
        ),
    )(*args)


def solution(mesh):
    placed = (P("row", "blk"), P("row", "blk"), P("row", "blk"), P(), P(), P(), P(), P(), P())
    return jax.shard_map(
        functools.partial(body, mesh.shape["blk"], mesh.shape["row"]),
        mesh=mesh,
        in_specs=placed,
        out_specs=(P("row", "blk"), P("row", "blk"), P("row", "blk")),
        check_vma=False,
    )
```

time: 292 us -> 123 us (0.42)
  waiting for transfers between devices: 248 us -> 0 us
  Pallas kernels: 0 us -> 113 us
  matrix products: 28.4 us -> 0 us
  between operations: 14.7 us -> 1.3 us
  local copies, waits for them, and re-layouts: 0.04 us -> 8.43 us
    all_gather x9 -> x0, waiting for transfers between devices: 247 us -> none  [the longest x1 31.7 us: body(): s_cols = lax.all_gather(seff, 'row', axis=0, tiled=True)]
    pallas_call x0 -> x1, Pallas kernels: none -> 113 us  [body(): pl.pallas_call(functools.partial(kernel, blks, rows_n), out_shape=(out, o...]
    dot_general x16 -> x0, matrix products: 28.4 us -> none  [the longest x4 13 us: make_folder(): return jnp.dot(panel, piece, preferred_element_type=jnp.float32)]
    unnamed x16 -> x19, local copies, waits for them, and re-layouts: 0.04 us -> 8.43 us
  transfers between devices with their start and end apart: 9 -> 0, of which waited for: 9 -> 0; matrix products, arithmetic and copies ran while one was open for 5% -> 0% of each run, Pallas kernels for 0% -> 0%
where the time goes in v1:
time: 123 us; the launch traced here: 122 us
  Pallas kernels  113 us (92%)
  local copies, waits for them, and re-layouts  8.43 us (7%)
  between operations  1.3 us (1%)
    pallas_call x1, Pallas kernels, body(): pl.pallas_call(functools.partial(kernel, blks, rows_n), out_shape=(out, o...  113 us
    unnamed x19, local copies, waits for them, and re-layouts  8.43 us

profile of v1, /device:TPU:1, one launch (start us, length us, event | category | flops | bytes accessed | tf_op | source)
XLA Modules:
  0.0 122.4 jit_solution(2661080952164132857)
XLA Ops:
  1.3 0.0 copy-start
  1.3 0.9 copy-done
  2.2 0.0 copy-start.1
  2.2 0.9 copy-done.1
  3.2 0.0 copy-start.2
  3.2 0.9 copy-done.2
  4.1 0.0 copy-start.3
  4.1 0.7 copy-done.3
  4.8 0.0 copy-start.4
  4.8 0.7 copy-done.4
  5.5 0.0 copy-start.5
  5.5 0.7 copy-done.5
  6.2 0.0 copy-start.6
  6.2 0.7 copy-done.6
  6.9 0.0 copy-start.7
  6.9 0.7 copy-done.7
  7.6 112.6 %shard_map.112 = (bf16[256,512]{1,0:T(8,128)(2,1)S(1)}, bf16[256,512]{1,0:T(8,128)(2,1)S(1)}, bf16[256,512]{1,0:T(8,128)(2,1)S(1)}) custom-call(bf16[256,512]{1,0:T(8,128)(2,1)S(1)} %copy-done, bf16[256,512]{1,0:T(8,128)(2,1)S(1)} %copy-done.1, bf16[256,512]{1,0:T(8,128)(2,1)S(1)} %copy-done.2, f32[1]{0:T(128)S(6)} %copy.15.chem_ref, ...), custom_call_target="tpu_custom_call" | custom-call | flops 3221225472 | bytes 1572864 | tf_op jit(solution)/shard_map/pallas_call | solution.py:326
  120.3 0.7 copy.16
  121.0 0.7 copy.17
  121.7 0.7 copy.18
Async XLA Ops:
  1.3 1.0 copy-start
  2.2 0.9 copy-start.1
  3.2 0.9 copy-start.2
  4.1 0.7 copy-start.3
  4.8 0.7 copy-start.4
  5.5 0.7 copy-start.5
  6.2 0.7 copy-start.6
  6.9 0.7 copy-start.7

commit v2 on v1

--- a/solution.py
+++ b/solution.py
@@ -8,6 +8,7 @@
 from jax.sharding import PartitionSpec as P
 
 BS = 128
+PARTS = 4
 MESH = pl.DeviceIdType.MESH
 S, Z, H, X, Q = range(5)
 ZR, FR, RR, XR = range(4)
@@ -16,15 +17,15 @@
 def kernel(
     blks,
     rows_n,
-    inter_ref,
-    inv_ref,
-    ham_ref,
-    chem_ref,
-    ps_ref,
-    pz_ref,
-    ph_ref,
-    fi_ref,
-    fs_ref,
+    inter_hbm,
+    inv_hbm,
+    ham_hbm,
+    chem_hbm,
+    ps_hbm,
+    pz_hbm,
+    ph_hbm,
+    fi_hbm,
+    fs_hbm,
     refined_ref,
     error_ref,
     sign_ref,
@@ -35,7 +36,35 @@
     col_recv,
     row_send,
     row_recv,
+    inter_ref,
+    inv_ref,
+    ham_ref,
+    chem_ref,
+    ps_ref,
+    pz_ref,
+    ph_ref,
+    fi_ref,
+    fs_ref,
+    load_sem,
 ):
+    loads = [
+        pltpu.make_async_copy(source, target, load_sem.at[n])
+        for n, (source, target) in enumerate(
+            (
+                (inter_hbm, inter_ref),
+                (ps_hbm, ps_ref),
+                (inv_hbm, inv_ref),
+                (pz_hbm, pz_ref),
+                (ham_hbm, ham_ref),
+                (ph_hbm, ph_ref),
+                (fi_hbm, fi_ref),
+                (fs_hbm, fs_ref),
+                (chem_hbm, chem_ref),
+            )
+        )
+    ]
+    for load in loads:
+        load.start()
     rows, width = inter_ref.shape
     chips = rows_n // 2
     chunk = 2 * rows
@@ -52,15 +81,17 @@
     def blk_device(b):
         return {"row": me_row, "blk": b}
 
-    def slot(i, r):
-        return cols.at[i, pl.ds(pl.multiple_of(r * rows, rows), rows)]
-
-    def col_copy(i, kind, c, target, source):
+    piece = rows // PARTS
+
+    def slot(i, r, part):
+        return cols.at[i, pl.ds(pl.multiple_of(r * rows + part * piece, piece), piece)]
+
+    def col_copy(i, kind, c, target, source, part):
         return pltpu.make_async_remote_copy(
-            src_ref=slot(i, source),
-            dst_ref=slot(i, source),
-            send_sem=col_send.at[i, kind, c],
-            recv_sem=col_recv.at[i, source],
+            src_ref=slot(i, source, part),
+            dst_ref=slot(i, source, part),
+            send_sem=col_send.at[i, kind, c, part],
+            recv_sem=col_recv.at[i, source, part],
             device_id=row_device(target),
             device_id_type=MESH,
         )
@@ -68,17 +99,18 @@
     def mine(c):
         return c * 2 + core
 
-    def up(i, c):
-        return col_copy(i, 0, c, me_row + 2, mine(c))
-
-    def down(i, c):
-        return col_copy(i, 1, c, me_row - 2, mine(c))
-
-    def across(i, c):
-        return col_copy(i, 2, c, mate, mine(c))
+    def up(i, c, part):
+        return col_copy(i, 0, c, me_row + 2, mine(c), part)
+
+    def down(i, c, part):
+        return col_copy(i, 1, c, me_row - 2, mine(c), part)
+
+    def across(i, c, part):
+        return col_copy(i, 2, c, mate, mine(c), part)
 
     def from_mate(i, c):
-        return col_copy(i, 2, c, mate, c * 2 + (1 - core))
+        for part in range(PARTS):
+            col_copy(i, 2, c, mate, c * 2 + (1 - core), part).wait_recv()
 
     def row_copy(i, step):
         to = lax.rem(me_blk + step, blks)
@@ -111,38 +143,43 @@
             row_arrival(i, step).wait_recv()
 
     def send_own(i):
-        @pl.when(chip + 1 < chips)
-        def _():
-            up(i, chip).start()
-
-        @pl.when(chip > 0)
-        def _():
-            down(i, chip).start()
-
-        across(i, chip).start()
-
-    def relay(i, d):
-        @pl.when(chip - d >= 0)
-        def _():
-            c = chip - d
-            up(i, c).wait_recv()
+        for part in range(PARTS):
 
             @pl.when(chip + 1 < chips)
             def _():
-                up(i, c).start()
-
-            across(i, c).start()
-
-        @pl.when(chip + d < chips)
-        def _():
-            c = chip + d
-            down(i, c).wait_recv()
+                up(i, chip, part).start()
 
             @pl.when(chip > 0)
             def _():
-                down(i, c).start()
-
-            across(i, c).start()
+                down(i, chip, part).start()
+
+        for part in range(PARTS):
+            across(i, chip, part).start()
+
+    def relay(i, d):
+        for part in range(PARTS):
+
+            @pl.when(chip - d >= 0)
+            def _():
+                c = chip - d
+                up(i, c, part).wait_recv()
+
+                @pl.when(chip + 1 < chips)
+                def _():
+                    up(i, c, part).start()
+
+                across(i, c, part).start()
+
+            @pl.when(chip + d < chips)
+            def _():
+                c = chip + d
+                down(i, c, part).wait_recv()
+
+                @pl.when(chip > 0)
+                def _():
+                    down(i, c, part).start()
+
+                across(i, c, part).start()
 
     def term(i, a, c):
         left = panels[a, c // per] if per == 1 else panels[a, c // per, :, pl.ds(pl.multiple_of(c % per * chunk, chunk), chunk)]
@@ -153,13 +190,13 @@
         @pl.when(chip - d >= 0)
         def _():
             c = chip - d
-            from_mate(i, c).wait_recv()
+            from_mate(i, c)
             acc[...] += term(i, a, c)
 
         @pl.when(chip + d < chips)
         def _():
             c = chip + d
-            from_mate(i, c).wait_recv()
+            from_mate(i, c)
             acc[...] += term(i, a, c)
 
     def loop(low, high, f):
@@ -174,7 +211,7 @@
         after()
         if fresh:
             wait_rows(a)
-        from_mate(i, chip).wait_recv()
+        from_mate(i, chip)
         acc[...] = term(i, a, chip)
         loop(1, chips - 1, lambda d: fold(i, a, d))
         if chips > 1:
@@ -260,14 +297,21 @@
     def _():
         greet(row_device(me_row - 2))
 
+    def arrive(first, last):
+        for load in loads[first:last]:
+            load.wait()
+
+    arrive(0, 2)
     tiles(make_s)
-    tiles(make_z)
     above = jnp.where(chip + 1 < chips, 1, 0)
     below = jnp.where(chip > 0, 1, 0)
     pl.semaphore_wait(barrier, blks + above + below)
 
     send_own(S)
+    arrive(2, 4)
+    tiles(make_z)
     send_rows(ZR)
+    arrive(4, 9)
     tiles(make_h)
 
     column_pass(S, ZR, lambda: send_own(Z))
@@ -301,15 +345,17 @@
     for i in range(5):
 
         def drain(c, i=i):
-            @pl.when((chip + 1 < chips) & (c <= chip))
-            def _():
-                up(i, c).wait_send()
-
-            @pl.when((chip > 0) & (c >= chip))
-            def _():
-                down(i, c).wait_send()
-
-            across(i, c).wait_send()
+            for part in range(PARTS):
+
+                @pl.when((chip + 1 < chips) & (c <= chip))
+                def _():
+                    up(i, c, part).wait_send()
+
+                @pl.when((chip > 0) & (c >= chip))
+                def _():
+                    down(i, c, part).wait_send()
+
+                across(i, c, part).wait_send()
 
         loop(0, chips, drain)
     for i in range(4):
@@ -321,24 +367,26 @@
     rows, width = args[0].shape
     out = jax.ShapeDtypeStruct((rows, width), jnp.bfloat16)
     vmem = pl.BlockSpec(memory_space=pltpu.VMEM)
-    smem = pl.BlockSpec(memory_space=pltpu.SMEM)
     depth = rows_n * rows
     return pl.pallas_call(
         functools.partial(kernel, blks, rows_n),
         out_shape=(out, out, out),
-        in_specs=[vmem] * 3 + [smem] * 6,
+        in_specs=[pl.BlockSpec(memory_space=pl.ANY)] * 9,
         out_specs=(vmem, vmem, vmem),
         scratch_shapes=[
             pltpu.VMEM((5, depth, width), jnp.bfloat16),
             pltpu.VMEM((4, blks, rows, width), jnp.bfloat16),
             pltpu.VMEM((rows, width), jnp.float32),
-            pltpu.SemaphoreType.DMA((5, 3, rows_n // 2)),
-            pltpu.SemaphoreType.DMA((5, rows_n)),
+            pltpu.SemaphoreType.DMA((5, 3, rows_n // 2, PARTS)),
+            pltpu.SemaphoreType.DMA((5, rows_n, PARTS)),
             pltpu.SemaphoreType.DMA((4, blks)),
             pltpu.SemaphoreType.DMA((4, blks)),
+            *(pltpu.VMEM(a.shape, a.dtype) for a in args[:3]),
+            *(pltpu.SMEM(a.shape, a.dtype) for a in args[3:]),
+            pltpu.SemaphoreType.DMA((9,)),
         ],
         compiler_params=pltpu.CompilerParams(
-            collective_id=0, has_side_effects=True, vmem_limit_bytes=48 * 1024 * 1024
+            collective_id=0, has_side_effects=True, vmem_limit_bytes=60 * 1024 * 1024
         ),
         cost_estimate=pl.CostEstimate(
             flops=12 * rows * depth * width, bytes_accessed=12 * rows * width, transcendentals=0

time: 123 us -> 105 us (0.85)
  Pallas kernels: 113 us -> 100 us
  local copies, waits for them, and re-layouts: 8.43 us -> 3.46 us
    pallas_call x1, Pallas kernels: 113 us -> 100 us  [body(): pl.pallas_call(functools.partial(kernel, blks, rows_n), out_shape=(out, o...]
    unnamed x19 -> x7, local copies, waits for them, and re-layouts: 8.43 us -> 3.46 us
where the time goes in v2:
time: 105 us
  Pallas kernels  100 us (95%)
  local copies, waits for them, and re-layouts  3.46 us (3%)
  between operations  1.3 us (1%)
    pallas_call x1, Pallas kernels, body(): pl.pallas_call(functools.partial(kernel, blks, rows_n), out_shape=(out, o...  100 us
    unnamed x7, local copies, waits for them, and re-layouts  3.46 us

profile of v2, /device:TPU:1, one launch (start us, length us, event | category | flops | bytes accessed | tf_op | source)
XLA Modules:
  0.0 104.8 jit_solution(1467793930015890105)
XLA Ops:
  1.3 100.0 %shard_map.112 = (bf16[256,512]{1,0:T(8,128)(2,1)}, bf16[256,512]{1,0:T(8,128)(2,1)}, bf16[256,512]{1,0:T(8,128)(2,1)}) custom-call(bf16[256,512]{1,0:T(8,128)(2,1)} %inter_hbm.1, bf16[256,512]{1,0:T(8,128)(2,1)} %inv_hbm.1, bf16[256,512]{1,0:T(8,128)(2,1)} %ham_hbm.1, f32[1]{0:T(128)S(6)} %copy.15.chem_hbm, s32[16,16]{1,0:T(8,128)} %ps_hbm.1, ...), custom_call_target="tpu_custom_call" | custom-call | flops 3221225472 | bytes 1572864 | tf_op jit(solution)/shard_map/pallas_call | solution.py:371
  101.3 0.0 copy-start.1
  101.3 1.7 %copy.16 = bf16[256,512]{1,0:T(8,128)(2,1)} copy(bf16[256,512]{1,0:T(8,128)(2,1)} %get-tuple-element.6) | data formatting | bytes 524288
  103.0 0.0 copy-done.1
  103.0 0.0 copy-start
  103.0 0.7 copy.17
  103.7 0.3 copy-done
  104.1 0.7 copy.18
Async XLA Ops:
  101.3 1.7 %copy-start.1 = (bf16[256,512]{1,0:T(8,128)(2,1)S(1)}, bf16[256,512]{1,0:T(8,128)(2,1)}, u32[]{:S(2)}) copy-start(bf16[256,512]{1,0:T(8,128)(2,1)} %get-tuple-element.7) | copy-start | bytes 786436
  103.0 1.0 copy-start

commit v3 on v2

--- a/solution.py
+++ b/solution.py
@@ -363,12 +363,17 @@
             row_copy(i, step).wait_send()
 
 
+def hand_on(*refs):
+    for source, target in zip(refs[:3], refs[3:]):
+        target[...] = source[...]
+
+
 def body(blks, rows_n, *args):
     rows, width = args[0].shape
     out = jax.ShapeDtypeStruct((rows, width), jnp.bfloat16)
     vmem = pl.BlockSpec(memory_space=pltpu.VMEM)
     depth = rows_n * rows
-    return pl.pallas_call(
+    results = pl.pallas_call(
         functools.partial(kernel, blks, rows_n),
         out_shape=(out, out, out),
         in_specs=[pl.BlockSpec(memory_space=pl.ANY)] * 9,
@@ -392,6 +397,12 @@
             flops=12 * rows * depth * width, bytes_accessed=12 * rows * width, transcendentals=0
         ),
     )(*args)
+    return pl.pallas_call(
+        hand_on,
+        out_shape=(out, out, out),
+        in_specs=[vmem] * 3,
+        out_specs=(vmem, vmem, vmem),
+    )(*results)
 
 
 def solution(mesh):

time: 105 us -> 103 us (0.981)
  local copies, waits for them, and re-layouts: 3.46 us -> 0 us
  Pallas kernels: 100 us -> 102 us
    unnamed x7 -> x0, local copies, waits for them, and re-layouts: 3.46 us -> none
    pallas_call x0 -> x1, Pallas kernels: none -> 2 us  [body(): pl.pallas_call(hand_on, out_shape=(out, out, out), in_specs=[vmem] * 3, o...]
where the time goes in v3:
time: 103 us
  Pallas kernels  102 us (99%)
  between operations  1.29 us (1%)
    pallas_call x1, Pallas kernels, body(): pl.pallas_call(functools.partial(kernel, blks, rows_n), out_shape=(out, o...  100 us

profile of v3, /device:TPU:1, one launch (start us, length us, event | category | flops | bytes accessed | tf_op | source)
XLA Modules:
  0.0 103.3 jit_solution(8293839470198349030)
XLA Ops:
  1.3 100.0 %shard_map.112 = (bf16[256,512]{1,0:T(8,128)(2,1)}, bf16[256,512]{1,0:T(8,128)(2,1)}, bf16[256,512]{1,0:T(8,128)(2,1)}) custom-call(bf16[256,512]{1,0:T(8,128)(2,1)} %inter_hbm.1, bf16[256,512]{1,0:T(8,128)(2,1)} %inv_hbm.1, bf16[256,512]{1,0:T(8,128)(2,1)} %ham_hbm.1, f32[1]{0:T(128)S(6)} %copy.12.chem_hbm, s32[16,16]{1,0:T(8,128)} %ps_hbm.1, ...), custom_call_target="tpu_custom_call" | custom-call | flops 3221225472 | bytes 1572864 | tf_op jit(solution)/shard_map/pallas_call | solution.py:376
  101.3 2.0 %shard_map.113 = (bf16[256,512]{1,0:T(8,128)(2,1)}, bf16[256,512]{1,0:T(8,128)(2,1)}, bf16[256,512]{1,0:T(8,128)(2,1)}) custom-call(bf16[256,512]{1,0:T(8,128)(2,1)} %get-tuple-element.6.refs_0_, bf16[256,512]{1,0:T(8,128)(2,1)} %get-tuple-element.7.refs_1_, bf16[256,512]{1,0:T(8,128)(2,1)} %get-tuple-element.8.refs_2_), custom_call_target="tpu_custom_call" | custom-call | tf_op jit(solution)/shard_map/pallas_call | solution.py:400
